TPU v7x, 32 devices: a whole 2x2x4 slice. The times are simulated.
32 devices in a mesh: layer: 4 (over y, x), phi: 8 (over z, core).
Axes of the slice: x: 2, y: 2, z: 4, core: 2. Of those that a mesh axis runs over, the one named last changes fastest.
Arguments:
- hits: bfloat16 [4, 8, 8192, 128], P('layer', 'phi'), may hold values from -6 to 6
- attach_index: int32 [4, 8, 4, 8192], P('layer', 'phi'), may hold values from 0 to 1023, as said below
- attach_weight: bfloat16 [4, 8, 4, 8192], P('layer', 'phi'), may hold values from 0.049804688 to 1
- shard_counts: int32 [4, 8], P('layer', 'phi'), may hold values from 1024 to 8192, as said below
- edge_source: int32 [8, 8, 1024], P('phi'), may hold values from 0 to 2047
- cotangent: bfloat16 [8, 1024, 128], P('phi'), may hold values from -12 to 12
- w_message: bfloat16 [128, 128], replicated, may hold values from -0.5 to 0.5
- w_edge: bfloat16 [128, 128], replicated, may hold values from -0.5 to 0.5
- w_output: bfloat16 [128, 128], replicated, may hold values from -0.5 to 0.5
Outputs:
- d_hits: bfloat16 [4, 8, 8192, 128], P('layer', 'phi')
- grad_message: float32 [128, 128], replicated
- grad_edge: float32 [128, 128], replicated
- grad_output: float32 [128, 128], replicated
Inputs may be any that keep to these rules, and one draw needn't show every extreme that they name: `attach_index`: A hit's four super-nodes are different. `shard_counts`: slots from the count on are padding; at least one shard is full. `edge_source`: row r of a sector's extended list is the previous sector's super-node 1024 - 512 + r for r < 512, its own super-node r - 512 below 1536, and else the next sector's super-node r - 1536.
All inputs are finite; a program needn't handle non-finite values.
Results may differ from a plain program's by a relative error of at most 0.015.
Values may be sent and summed in bfloat16 or wider, within the bound.
A program may use at most 64 MiB of HBM per device.

v0:
```python
import math
import jax
import jax.numpy as jnp
from jax import lax
from jax.sharding import PartitionSpec as P


def with_halo(cells, sides, width):
    for axis, dim in sides:
        count = lax.axis_size(axis)
        head = lax.slice_in_dim(cells, 0, width, axis=dim)
        tail = lax.slice_in_dim(cells, cells.shape[dim] - width, cells.shape[dim], axis=dim)
        cells = jnp.concatenate(
            [
                lax.ppermute(tail, axis, [(i, (i + 1) % count) for i in range(count)]),
                cells,
                lax.ppermute(head, axis, [((i + 1) % count, i) for i in range(count)]),
            ],
            axis=dim,
        )
    return cells


def one_hot_tile(node_iota, index_blk, weight_blk):
    zero_value = jnp.zeros((), jnp.bfloat16)
    tile_sum = jnp.where(node_iota == index_blk[0][None, :], weight_blk[0][None, :], zero_value)
    for slot in range(1, index_blk.shape[0]):
        tile_sum = tile_sum + jnp.where(
            node_iota == index_blk[slot][None, :], weight_blk[slot][None, :], zero_value
        )
    return tile_sum


def normalize(totals, masses):
    scale = (1.0 / jnp.sqrt(1.0 + masses)).astype(jnp.bfloat16)
    node = (totals * scale.astype(jnp.float32)[:, None]).astype(jnp.bfloat16)
    return (node, scale)


def contract_rows(left, right):
    return lax.dot_general(
        left, right, (((0,), (0,)), ((), ())), preferred_element_type=jnp.float32
    )


def shards(
    hits,
    attach_index,
    attach_weight,
    shard_counts,
    edge_source,
    cotangent,
    w_message,
    w_edge,
    w_output,
):
    hit_block = hits[0, 0]
    hit_rows = hit_block.shape[0]
    features = hit_block.shape[1]
    nodes = cotangent.shape[1]
    rim_rows = nodes // 2
    layer_count = lax.axis_size("layer")
    sector_count = lax.axis_size("phi")
    share_rows = nodes // layer_count
    block_rows = min(512, hit_rows)
    block_count = hit_rows // block_rows
    grad_cot = cotangent[0]
    sources = edge_source[0]
    positions = jnp.arange(hit_rows, dtype=jnp.int32)
    realness = (positions < shard_counts[0, 0]).astype(jnp.bfloat16)
    weight_table = attach_weight[0, 0] * realness[None, :]
    index_table = attach_index[0, 0]
    message = jnp.tanh(jnp.dot(hit_block, w_message, preferred_element_type=jnp.float32)).astype(
        jnp.bfloat16
    )
    node_iota = jnp.arange(nodes, dtype=jnp.int32)[:, None]
    index_blocks = jnp.transpose(index_table.reshape(4, block_count, block_rows), (1, 0, 2))
    weight_blocks = jnp.transpose(weight_table.reshape(4, block_count, block_rows), (1, 0, 2))
    message_blocks = message.reshape(block_count, block_rows, features)

    def pool_step(carry, inputs):
        totals, masses = carry
        index_blk, weight_blk, message_blk = inputs
        tile_now = one_hot_tile(node_iota, index_blk, weight_blk)
        totals = totals + jnp.dot(tile_now, message_blk, preferred_element_type=jnp.float32)
        masses = masses + jnp.sum(tile_now.astype(jnp.float32), axis=1)
        return ((totals, masses), None)

    start_carry = (jnp.zeros((nodes, features), jnp.float32), jnp.zeros((nodes,), jnp.float32))
    (pooled, masses), _ = lax.scan(
        pool_step, start_carry, (index_blocks, weight_blocks, message_blocks)
    )
    totals, mass_sum = lax.psum((pooled, masses), "layer")
    node, scale = normalize(totals, mass_sum)
    preact = jnp.dot(node, w_edge, preferred_element_type=jnp.float32)
    sigma = jax.nn.sigmoid(preact)
    edge_msg = (preact * sigma).astype(jnp.bfloat16)
    beside_all = with_halo(edge_msg[None], (("phi", 0),), 1)
    lower_rim = beside_all[0, nodes - rim_rows :]
    upper_rim = beside_all[2, :rim_rows]
    extended = jnp.concatenate([lower_rim, edge_msg, upper_rim], axis=0)
    ext_iota = jnp.arange(nodes + 2 * rim_rows, dtype=jnp.int32)[None, :, None]
    adjacency = jnp.sum((ext_iota == sources[:, None, :]).astype(jnp.float32), axis=0).astype(
        jnp.bfloat16
    )
    gathered = contract_rows(adjacency, extended).astype(jnp.bfloat16)
    d_gathered = jnp.dot(grad_cot, w_output.T, preferred_element_type=jnp.float32).astype(
        jnp.bfloat16
    )
    spread = jnp.dot(adjacency, d_gathered, preferred_element_type=jnp.float32)
    edges_back = jnp.stack([spread[:rim_rows], spread[nodes + rim_rows :]])[None]
    returned = with_halo(edges_back, (("phi", 0),), 1)
    from_upper = returned[2, 0]
    from_lower = returned[0, 1]
    d_edge = spread[rim_rows : rim_rows + nodes]
    d_edge = d_edge.at[nodes - rim_rows :].add(from_upper)
    d_edge = d_edge.at[:rim_rows].add(from_lower)
    d_pre = (d_edge * (sigma * (1.0 + preact * (1.0 - sigma)))).astype(jnp.bfloat16)
    back_node = jnp.dot(d_pre, w_edge.T, preferred_element_type=jnp.float32)
    d_node = (
        (grad_cot.astype(jnp.float32) + back_node) * scale.astype(jnp.float32)[:, None]
    ).astype(jnp.bfloat16)
    share_start = lax.axis_index("layer") * share_rows
    gathered_share = lax.dynamic_slice_in_dim(gathered, share_start, share_rows, 0)
    grad_share = lax.dynamic_slice_in_dim(grad_cot, share_start, share_rows, 0)
    node_share = lax.dynamic_slice_in_dim(node, share_start, share_rows, 0)
    d_pre_share = lax.dynamic_slice_in_dim(d_pre, share_start, share_rows, 0)
    output_term = contract_rows(gathered_share, grad_share)
    edge_term = contract_rows(node_share, d_pre_share)

    def back_step(carry, inputs):
        index_blk, weight_blk, message_blk = inputs
        tile_now = one_hot_tile(node_iota, index_blk, weight_blk)
        d_message = contract_rows(tile_now, d_node)
        message_f = message_blk.astype(jnp.float32)
        return (carry, (d_message * (1.0 - message_f * message_f)).astype(jnp.bfloat16))

    _, d_act_blocks = lax.scan(back_step, 0, (index_blocks, weight_blocks, message_blocks))
    d_act = d_act_blocks.reshape(hit_rows, features)
    d_hits = jnp.dot(d_act, w_message.T, preferred_element_type=jnp.float32).astype(jnp.bfloat16)
    message_term = contract_rows(hit_block, d_act)
    summed = lax.psum((message_term, edge_term, output_term), ("layer", "phi"))
    hit_norm = math.sqrt(layer_count * sector_count * hit_rows)
    node_norm = math.sqrt(sector_count * nodes)
    return (d_hits[None, None], summed[0] / hit_norm, summed[1] / node_norm, summed[2] / node_norm)


def solution(mesh):
    placed = (
        P("layer", "phi", None, None),
        P("layer", "phi", None, None),
        P("layer", "phi", None, None),
        P("layer", "phi"),
        P("phi", None, None),
        P("phi", None, None),
        P(),
        P(),
        P(),
    )
    return jax.shard_map(
        shards,
        mesh=mesh,
        in_specs=placed,
        out_specs=(P("layer", "phi", None, None), P(), P(), P()),
        check_vma=False,
    )
```

profile of v0, /device:TPU:8, one launch (start us, length us, event | category | flops | bytes accessed | tf_op | source)
XLA Modules:
  0.0 367.0 jit_solution(7830874262734797815)
XLA Ops:
  7.2 14.9 %convert_reduce_fusion.1 = bf16[2048,1024]{1,0:T(8,128)(2,1)} fusion(s32[8,1024]{1,0:T(8,128)} %bitcast.123), kind=kLoop, calls=%fused_computation.69 | loop fusion | flops 48234496 | bytes 4227072 | tf_op jit(solution)/shard_map/reduce_sum | solution.py:103
  22.1 3.7 %fusion.55 = f32[2048,128]{1,0:T(8,128)S(1)} fusion(bf16[2048,1024]{1,0:T(8,128)(2,1)} %convert_reduce_fusion.1, bf16[128,128]{1,0:T(8,128)(2,1)S(1)} %copy-done.5, bf16[1,1024,128]{2,1,0:T(8,128)(2,1)S(1)} %copy-done.2), kind=kOutput, calls=%fused_computation.80 | convolution fusion | flops 570556416 | bytes 5537792 | tf_op jit(solution)/shard_map/dot_general | solution.py:110
  30.0 77.8 %while.29 = (s32[]{:T(128)}, f32[1024,128]{1,0:T(8,128)}, f32[1024]{0:T(1024)S(1)}, s32[16,4,512]{2,1,0:T(4,128)}, bf16[16,4,512]{2,1,0:T(4,128)(2,1)S(1)}, /*in...) while((s32[]{:T(128)}, f32[1024,128]{1,0:T(8,128)}, ...), condition=%wide.region_3.4_spmd.clone.clone, body=%wide.region_1.3_spmd.clone.clone.sunk | while | flops 151782400 | bytes 1245884 | solution.py:90
  35.6 3.0 convolution_add_fusion.3
  40.5 3.0 convolution_add_fusion.3
  45.3 3.0 convolution_add_fusion.3
  50.2 3.0 convolution_add_fusion.3
  55.1 3.0 convolution_add_fusion.3
  60.0 3.0 convolution_add_fusion.3
  64.8 3.0 convolution_add_fusion.3
  69.7 3.0 convolution_add_fusion.3
  74.6 3.0 convolution_add_fusion.3
  79.5 3.0 convolution_add_fusion.3
  84.3 3.0 convolution_add_fusion.3
  89.2 3.0 convolution_add_fusion.3
  94.1 3.0 convolution_add_fusion.3
  99.0 3.0 convolution_add_fusion.3
  103.8 3.0 convolution_add_fusion.3
  107.9 9.9 %psum.36 = f32[1024]{0:T(1024)S(1)} all-reduce(f32[1024]{0:T(1024)S(1)} %get-tuple-element.122), channel_id=1, replica_groups=mesh['layer'=4,'phi'=8] {'layer'}, use_global_device_ids=true, to_apply=%region_5.6 | all-reduce | flops 1024 | bytes 8192 | tf_op jit(solution)/shard_map/psum | solution.py:93
  122.1 34.9 %all-reduce.4.cloned.1.call-done = f32[1024,128]{1,0:T(8,128)} async-done(((f32[1024,128]{1,0:T(8,128)}), f32[1024,128]{1,0:T(8,128)}) %all-reduce.4.cloned.1.call-update) | async-done | bytes 524304 | tf_op jit(solution)/shard_map/psum | solution.py:93
  161.2 59.3 %while.28 = (s32[]{:T(128)}, bf16[16,512,128]{2,1,0:T(8,128)(2,1)}, s32[16,4,512]{2,1,0:T(4,128)}, bf16[16,4,512]{2,1,0:T(4,128)(2,1)S(1)}, bf16[1024,128]{1,0:T...) while((s32[]{:T(128)}, bf16[16,512,128]{2,1,0:T(8,128)(2,1)}, ...), condition=%wide.region_7.8_spmd.clone.clone, body=%wide.region_6.7_spmd.clone.clone.sunk | while | flops 142934016 | bytes 561841 | solution.py:138
  220.4 3.1 fusion.59
  228.5 3.6 fusion.49
  232.1 125.0 %all-reduce.6.cloned.1.call-done = (f32[128,128]{0,1:T(8,128)}, f32[128,128]{1,0:T(8,128)}, f32[128,128]{1,0:T(8,128)}) async-done(((f32[128,128]{0,1:T(8,128)}, f32[128,128]{1,0:T(8,128)}, f32[128,128]{1,0:T(8,128)}), (f32[128,128]{0,1:T(8,128)}, f32[128,128]{1,0:T(8,128)}, f32[128,128]{1,0:T(8,128)})) %all-reduce.6.cloned.1.call-update) | async-done | bytes 196624 | tf_op jit(solution)/shard_map/psum | solution.py:142
  (162 shorter events, 111.2 us)
Async XLA Ops:
  7.2 20.8 %copy-start = (bf16[1,1,8192,128]{3,2,1,0:T(8,128)(2,1)S(1)}, bf16[1,1,8192,128]{3,2,1,0:T(8,128)(2,1)}, u32[]{:S(2)}) copy-start(bf16[1,1,8192,128]{3,2,1,0:T(8,128)(2,1)} %param.17) | copy-start | bytes 6291460
  7.2 149.8 %all-reduce.4.cloned.1.call-start = ((), (), s32[]{:S(2)}) async-start(), calls=%async_computation | async-start | bytes 1048576 | tf_op jit(solution)/shard_map/psum | solution.py:93
  7.2 14.9 %copy-start.2 = (bf16[1,1024,128]{2,1,0:T(8,128)(2,1)S(1)}, bf16[1,1024,128]{2,1,0:T(8,128)(2,1)}, u32[]{:S(2)}) copy-start(bf16[1,1024,128]{2,1,0:T(8,128)(2,1)} %param.22) | copy-start | bytes 786436
  7.2 14.9 %copy-start.5 = (bf16[128,128]{1,0:T(8,128)(2,1)S(1)}, bf16[128,128]{1,0:T(8,128)(2,1)}, u32[]{:S(2)}) copy-start(bf16[128,128]{1,0:T(8,128)(2,1)} %param.25) | copy-start | bytes 98308
  25.8 2.1 copy-start.3
  26.7 91.9 %collective-permute-start = (f32[1,2,512,128]{3,2,1,0:T(8,128)}, f32[1,2,512,128]{3,2,1,0:T(8,128)}, u32[]{:S(2)}, u32[]{:S(2)}) collective-permute-start(f32[1,2,512,128]{3,2,1,0:T(8,128)} %maximum_bitcast_fusion), channel_id=1, source_target_pairs={{1,0},{2,1},{3,2},{4,3},{5,4},{6,5},{7,6},{0,7},{9,8},{10,9},{11,1... | collective-permute-start | bytes 1572872 | tf_op jit(solution)/shard_map/ppermute | solution.py:17
  26.7 93.6 %collective-permute-start.1 = (f32[1,2,512,128]{3,2,1,0:T(8,128)}, f32[1,2,512,128]{3,2,1,0:T(8,128)}, u32[]{:S(2)}, u32[]{:S(2)}) collective-permute-start(f32[1,2,512,128]{3,2,1,0:T(8,128)} %maximum_bitcast_fusion), channel_id=1, source_target_pairs={{0,1},{1,2},{2,3},{3,4},{4,5},{5,6},{6,7},{7,0},{8,9},{9,10},{10,1... | collective-permute-start | bytes 1572872 | tf_op jit(solution)/shard_map/ppermute | solution.py:15
  27.9 2.0 copy-start.4
  107.8 50.5 %copy-start.6 = (bf16[128,128]{1,0:T(8,128)(2,1)S(1)}, bf16[128,128]{1,0:T(8,128)(2,1)}, u32[]{:S(2)}) copy-start(bf16[128,128]{1,0:T(8,128)(2,1)} %param.24) | copy-start | bytes 98308
  107.8 249.2 %all-reduce.6.cloned.1.call-start = ((), (), s32[]{:S(2)}) async-start(), calls=%async_computation.1 | async-start | bytes 393216 | tf_op jit(solution)/shard_map/psum | solution.py:142
  160.4 64.0 %collective-permute-start.3 = (bf16[1,1024,128]{2,1,0:T(8,128)(2,1)}, bf16[1,1024,128]{2,1,0:T(8,128)(2,1)}, u32[]{:S(2)}, u32[]{:S(2)}) collective-permute-start(bf16[1,1024,128]{2,1,0:T(8,128)(2,1)} %bitcast.18), channel_id=1, source_target_pairs={{1,0},{2,1},{3,2},{4,3},{5,4},{6,5},{7,6},{0,7},{9,8},{10,9},{11,1... | collective-permute-start | bytes 786440 | tf_op jit(solution)/shard_map/ppermute | solution.py:17
  160.4 64.9 %collective-permute-start.2 = (bf16[1,1024,128]{2,1,0:T(8,128)(2,1)}, bf16[1,1024,128]{2,1,0:T(8,128)(2,1)S(1)}, u32[]{:S(2)}, u32[]{:S(2)}) collective-permute-start(bf16[1,1024,128]{2,1,0:T(8,128)(2,1)} %bitcast.18), channel_id=1, source_target_pairs={{0,1},{1,2},{2,3},{3,4},{4,5},{5,6},{6,7},{7,0},{8,9},{9,10},{10,1... | collective-permute-start | bytes 786440 | tf_op jit(solution)/shard_map/ppermute | solution.py:15
  220.4 4.9 %copy-start.1 = (bf16[2048,1024]{1,0:T(8,128)(2,1)S(1)}, bf16[2048,1024]{1,0:T(8,128)(2,1)}, u32[]{:S(2)}) copy-start(bf16[2048,1024]{1,0:T(8,128)(2,1)} %convert_reduce_fusion.1) | copy-start | bytes 12582916
Sparse Core Ops, SparseCore 0:
  107.9 49.0 all-reduce.3
  228.6 128.4 all-reduce.5
where the time goes:
time: 370 us; the launch traced here: 367 us
  waiting for transfers between devices  160 us (43%)
  matrix products  112 us (30%)
  other arithmetic  37.5 us (10%)
  local copies, waits for them, and re-layouts  31.6 us (9%)
  between operations  14.8 us (4%)
  blocking collectives  9.91 us (3%)
    psum x1, waiting for transfers between devices, shards(): summed = lax.psum((message_term, edge_term, output_term), ('layer', 'phi'))  125 us
    dot_general x20, matrix products, contract_rows(): lax.dot_general(left, right, (((0,), (0,)), ((), ())), preferred_element_...  51.8 us
    dot_general x16, matrix products, pool_step(): jnp.dot(tile_now, message_blk, preferred_element_type=jnp.float32)  48 us
    psum x1, waiting for transfers between devices, shards(): totals, mass_sum = lax.psum((pooled, masses), 'layer')  34.9 us
    slice x32, local copies, waits for them, and re-layouts, one_hot_tile(): index_blk[0][None, :]  27.4 us
    reduce_sum x1, other arithmetic, shards(): jnp.sum((ext_iota == sources[:, None, :]).astype(jnp.float32), axis=0)  14.9 us
    reduce_sum x16, other arithmetic, pool_step(): masses = masses + jnp.sum(tile_now.astype(jnp.float32), axis=1)  14.5 us
    psum x1, blocking collectives, shards(): totals, mass_sum = lax.psum((pooled, masses), 'layer')  9.91 us
  transfers between devices with their start and end apart: 6, of which 2 were waited for; matrix products, arithmetic and copies ran while one was open for 41% of the time, Pallas kernels for 0%

commit v1 on v0

--- a/solution.py
+++ b/solution.py
@@ -139,7 +139,7 @@
     d_act = d_act_blocks.reshape(hit_rows, features)
     d_hits = jnp.dot(d_act, w_message.T, preferred_element_type=jnp.float32).astype(jnp.bfloat16)
     message_term = contract_rows(hit_block, d_act)
-    summed = lax.psum((message_term, edge_term, output_term), ("layer", "phi"))
+    summed = lax.psum(lax.psum((message_term, edge_term, output_term), "phi"), "layer")
     hit_norm = math.sqrt(layer_count * sector_count * hit_rows)
     node_norm = math.sqrt(sector_count * nodes)
     return (d_hits[None, None], summed[0] / hit_norm, summed[1] / node_norm, summed[2] / node_norm)

time: 370 us -> 346 us (0.935)
  waiting for transfers between devices: 160 us -> 134 us
    psum x1 -> x2, waiting for transfers between devices: 125 us -> 99.3 us  [the longest x1 56.4 us: shards(): lax.psum((message_term, edge_term, output_term), 'phi')]
  transfers between devices with their start and end apart: 6 -> 7, of which waited for: 2 -> 3; matrix products, arithmetic and copies ran while one was open for 41% -> 44% of each run, Pallas kernels for 0% -> 0%
where the time goes in v1:
time: 346 us; the launch traced here: 341 us
  waiting for transfers between devices  134 us (39%)
  matrix products  112 us (32%)
  other arithmetic  37.5 us (11%)
  local copies, waits for them, and re-layouts  31.6 us (9%)
  between operations  14.6 us (4%)
  blocking collectives  9.91 us (3%)
    psum x1, waiting for transfers between devices, shards(): lax.psum((message_term, edge_term, output_term), 'phi')  56.4 us
    dot_general x20, matrix products, contract_rows(): lax.dot_general(left, right, (((0,), (0,)), ((), ())), preferred_element_...  51.8 us
    dot_general x16, matrix products, pool_step(): jnp.dot(tile_now, message_blk, preferred_element_type=jnp.float32)  48 us
    psum x1, waiting for transfers between devices, shards(): lax.psum(lax.psum((message_term, edge_term, output_term), 'phi'), 'layer')  42.9 us
    psum x1, waiting for transfers between devices, shards(): totals, mass_sum = lax.psum((pooled, masses), 'layer')  34.9 us
    slice x32, local copies, waits for them, and re-layouts, one_hot_tile(): index_blk[0][None, :]  27.4 us
    reduce_sum x1, other arithmetic, shards(): jnp.sum((ext_iota == sources[:, None, :]).astype(jnp.float32), axis=0)  14.9 us
    reduce_sum x16, other arithmetic, pool_step(): masses = masses + jnp.sum(tile_now.astype(jnp.float32), axis=1)  14.5 us
  transfers between devices with their start and end apart: 7, of which 3 were waited for; matrix products, arithmetic and copies ran while one was open for 44% of the time, Pallas kernels for 0%

profile of v1, /device:TPU:8, one launch (start us, length us, event | category | flops | bytes accessed | tf_op | source)
XLA Modules:
  0.0 341.1 jit_solution(10467985407188185740)
XLA Ops:
  7.2 14.9 %convert_reduce_fusion.1 = bf16[2048,1024]{1,0:T(8,128)(2,1)} fusion(s32[8,1024]{1,0:T(8,128)} %bitcast.123), kind=kLoop, calls=%fused_computation.69 | loop fusion | flops 48234496 | bytes 4227072 | tf_op jit(solution)/shard_map/reduce_sum | solution.py:103
  22.1 3.7 %fusion.55 = f32[2048,128]{1,0:T(8,128)S(1)} fusion(bf16[2048,1024]{1,0:T(8,128)(2,1)} %convert_reduce_fusion.1, bf16[128,128]{1,0:T(8,128)(2,1)S(1)} %copy-done.5, bf16[1,1024,128]{2,1,0:T(8,128)(2,1)S(1)} %copy-done.2), kind=kOutput, calls=%fused_computation.80 | convolution fusion | flops 570556416 | bytes 5537792 | tf_op jit(solution)/shard_map/dot_general | solution.py:110
  30.0 77.8 %while.29 = (s32[]{:T(128)}, f32[1024,128]{1,0:T(8,128)}, f32[1024]{0:T(1024)S(1)}, s32[16,4,512]{2,1,0:T(4,128)}, bf16[16,4,512]{2,1,0:T(4,128)(2,1)S(1)}, /*in...) while((s32[]{:T(128)}, f32[1024,128]{1,0:T(8,128)}, ...), condition=%wide.region_3.4_spmd.clone.clone, body=%wide.region_1.3_spmd.clone.clone.sunk | while | flops 151782400 | bytes 1245884 | solution.py:90
  35.6 3.0 convolution_add_fusion.3
  40.5 3.0 convolution_add_fusion.3
  45.3 3.0 convolution_add_fusion.3
  50.2 3.0 convolution_add_fusion.3
  55.1 3.0 convolution_add_fusion.3
  60.0 3.0 convolution_add_fusion.3
  64.8 3.0 convolution_add_fusion.3
  69.7 3.0 convolution_add_fusion.3
  74.6 3.0 convolution_add_fusion.3
  79.5 3.0 convolution_add_fusion.3
  84.3 3.0 convolution_add_fusion.3
  89.2 3.0 convolution_add_fusion.3
  94.1 3.0 convolution_add_fusion.3
  103.8 3.0 convolution_add_fusion.3
  107.9 9.9 %psum.57 = f32[1024]{0:T(1024)S(1)} all-reduce(f32[1024]{0:T(1024)S(1)} %get-tuple-element.122), channel_id=1, replica_groups=mesh['layer'=4,'phi'=8] {'layer'}, use_global_device_ids=true, to_apply=%region_5.6 | all-reduce | flops 1024 | bytes 8192 | tf_op jit(solution)/shard_map/psum | solution.py:93
  122.1 34.9 %all-reduce.6.cloned.1.call-done = f32[1024,128]{1,0:T(8,128)} async-done(((f32[1024,128]{1,0:T(8,128)}), f32[1024,128]{1,0:T(8,128)}) %all-reduce.6.cloned.1.call-update) | async-done | bytes 524304 | tf_op jit(solution)/shard_map/psum | solution.py:93
  161.2 59.3 %while.28 = (s32[]{:T(128)}, bf16[16,512,128]{2,1,0:T(8,128)(2,1)}, s32[16,4,512]{2,1,0:T(4,128)}, bf16[16,4,512]{2,1,0:T(4,128)(2,1)S(1)}, bf16[1024,128]{1,0:T...) while((s32[]{:T(128)}, bf16[16,512,128]{2,1,0:T(8,128)(2,1)}, ...), condition=%wide.region_7.8_spmd.clone.clone, body=%wide.region_6.7_spmd.clone.clone.sunk | while | flops 142934016 | bytes 561841 | solution.py:138
  220.4 3.1 fusion.59
  228.5 56.4 %all-reduce.8.cloned.1.call-done = (f32[128,128]{0,1:T(8,128)}, f32[128,128]{1,0:T(8,128)}, f32[128,128]{1,0:T(8,128)}) async-done(((f32[128,128]{0,1:T(8,128)}, f32[128,128]{1,0:T(8,128)}, f32[128,128]{1,0:T(8,128)}), (f32[128,128]{0,1:T(8,128)}, f32[128,128]{1,0:T(8,128)}, f32[128,128]{1,0:T(8,128)})) %all-reduce.8.cloned.1.call-update) | async-done | bytes 196624 | tf_op jit(solution)/shard_map/psum | solution.py:142
  285.0 3.6 %fusion.49 = bf16[1,1,8192,128]{3,2,1,0:T(8,128)(2,1)} fusion(bf16[8192,128]{1,0:T(8,128)(2,1)} %bitcast.107, bf16[128,128]{1,0:T(8,128)(2,1)S(1)} %copy-done.3), kind=kOutput, calls=%fused_computation.74 | convolution fusion | flops 269484032 | bytes 4227072 | tf_op jit(solution)/shard_map/dot_general | solution.py:140
  288.6 42.9 %all-reduce.10.cloned.1.call-done = (f32[128,128]{0,1:T(8,128)}, f32[128,128]{1,0:T(8,128)}, f32[128,128]{1,0:T(8,128)}) async-done(((f32[128,128]{0,1:T(8,128)}, f32[128,128]{1,0:T(8,128)}, f32[128,128]{1,0:T(8,128)}), (f32[128,128]{0,1:T(8,128)}, f32[128,128]{1,0:T(8,128)}, f32[128,128]{1,0:T(8,128)})) %all-reduce.10.cloned.1.call-update) | async-done | bytes 196624 | tf_op jit(solution)/shard_map/psum | solution.py:142
  (165 shorter events, 114.3 us)
Async XLA Ops:
  7.2 20.8 %copy-start = (bf16[1,1,8192,128]{3,2,1,0:T(8,128)(2,1)S(1)}, bf16[1,1,8192,128]{3,2,1,0:T(8,128)(2,1)}, u32[]{:S(2)}) copy-start(bf16[1,1,8192,128]{3,2,1,0:T(8,128)(2,1)} %param.17) | copy-start | bytes 6291460
  7.2 149.8 %all-reduce.6.cloned.1.call-start = ((), (), s32[]{:S(2)}) async-start(), calls=%async_computation | async-start | bytes 1048576 | tf_op jit(solution)/shard_map/psum | solution.py:93
  7.2 14.9 %copy-start.2 = (bf16[1,1024,128]{2,1,0:T(8,128)(2,1)S(1)}, bf16[1,1024,128]{2,1,0:T(8,128)(2,1)}, u32[]{:S(2)}) copy-start(bf16[1,1024,128]{2,1,0:T(8,128)(2,1)} %param.22) | copy-start | bytes 786436
  7.2 14.9 %copy-start.5 = (bf16[128,128]{1,0:T(8,128)(2,1)S(1)}, bf16[128,128]{1,0:T(8,128)(2,1)}, u32[]{:S(2)}) copy-start(bf16[128,128]{1,0:T(8,128)(2,1)} %param.25) | copy-start | bytes 98308
  25.8 2.1 copy-start.3
  26.7 91.9 %collective-permute-start = (f32[1,2,512,128]{3,2,1,0:T(8,128)}, f32[1,2,512,128]{3,2,1,0:T(8,128)}, u32[]{:S(2)}, u32[]{:S(2)}) collective-permute-start(f32[1,2,512,128]{3,2,1,0:T(8,128)} %maximum_bitcast_fusion), channel_id=1, source_target_pairs={{1,0},{2,1},{3,2},{4,3},{5,4},{6,5},{7,6},{0,7},{9,8},{10,9},{11,1... | collective-permute-start | bytes 1572872 | tf_op jit(solution)/shard_map/ppermute | solution.py:17
  26.7 93.6 %collective-permute-start.1 = (f32[1,2,512,128]{3,2,1,0:T(8,128)}, f32[1,2,512,128]{3,2,1,0:T(8,128)}, u32[]{:S(2)}, u32[]{:S(2)}) collective-permute-start(f32[1,2,512,128]{3,2,1,0:T(8,128)} %maximum_bitcast_fusion), channel_id=1, source_target_pairs={{0,1},{1,2},{2,3},{3,4},{4,5},{5,6},{6,7},{7,0},{8,9},{9,10},{10,1... | collective-permute-start | bytes 1572872 | tf_op jit(solution)/shard_map/ppermute | solution.py:15
  27.9 2.0 copy-start.4
  107.8 50.5 %copy-start.6 = (bf16[128,128]{1,0:T(8,128)(2,1)S(1)}, bf16[128,128]{1,0:T(8,128)(2,1)}, u32[]{:S(2)}) copy-start(bf16[128,128]{1,0:T(8,128)(2,1)} %param.24) | copy-start | bytes 98308
  107.8 177.1 %all-reduce.8.cloned.1.call-start = ((), (), s32[]{:S(2)}) async-start(), calls=%async_computation.1 | async-start | bytes 393216 | tf_op jit(solution)/shard_map/psum | solution.py:142
  160.4 64.0 %collective-permute-start.3 = (bf16[1,1024,128]{2,1,0:T(8,128)(2,1)}, bf16[1,1024,128]{2,1,0:T(8,128)(2,1)}, u32[]{:S(2)}, u32[]{:S(2)}) collective-permute-start(bf16[1,1024,128]{2,1,0:T(8,128)(2,1)} %bitcast.18), channel_id=1, source_target_pairs={{1,0},{2,1},{3,2},{4,3},{5,4},{6,5},{7,6},{0,7},{9,8},{10,9},{11,1... | collective-permute-start | bytes 786440 | tf_op jit(solution)/shard_map/ppermute | solution.py:17
  160.4 64.9 %collective-permute-start.2 = (bf16[1,1024,128]{2,1,0:T(8,128)(2,1)}, bf16[1,1024,128]{2,1,0:T(8,128)(2,1)S(1)}, u32[]{:S(2)}, u32[]{:S(2)}) collective-permute-start(bf16[1,1024,128]{2,1,0:T(8,128)(2,1)} %bitcast.18), channel_id=1, source_target_pairs={{0,1},{1,2},{2,3},{3,4},{4,5},{5,6},{6,7},{7,0},{8,9},{9,10},{10,1... | collective-permute-start | bytes 786440 | tf_op jit(solution)/shard_map/ppermute | solution.py:15
  220.4 4.9 %copy-start.1 = (bf16[2048,1024]{1,0:T(8,128)(2,1)S(1)}, bf16[2048,1024]{1,0:T(8,128)(2,1)}, u32[]{:S(2)}) copy-start(bf16[2048,1024]{1,0:T(8,128)(2,1)} %convert_reduce_fusion.1) | copy-start | bytes 12582916
  228.5 103.0 %all-reduce.10.cloned.1.call-start = ((), (), s32[]{:S(2)}) async-start(), calls=%async_computation.2 | async-start | bytes 393216 | tf_op jit(solution)/shard_map/psum | solution.py:142
Sparse Core Ops, SparseCore 0:
  107.9 49.0 all-reduce.5
  228.6 56.2 all-reduce.7
  288.4 43.0 all-reduce.9
